TPU v7x, 32 devices: a whole 2x2x4 slice. The times are simulated.
32 devices in a mesh: src: 8 (over z, core), tgt: 4 (over y, x).
Axes of the slice: x: 2, y: 2, z: 4, core: 2. Of those that a mesh axis runs over, the one named last changes fastest.
Arguments:
- src_emb: bfloat16 [8192, 768], P(('src', 'tgt')), may hold values from -0.05119037 to 0.05119037
- right_sentence_vectors: bfloat16 [4096, 768], P(('tgt', 'src')), may hold values from -0.05119037 to 0.05119037
- src_mass: float32 [8192], P('src'), may hold values from 0.25 to 4
- tgt_mass: float32 [4096], P('tgt'), may hold values from 0.5 to 8
Outputs:
- grad_src: float32 [8192, 768], P(('src', 'tgt'))
- grad_tgt: float32 [4096, 768], P(('tgt', 'src'))
All inputs are finite; a program needn't handle non-finite values.
Results may differ from a plain program's by a relative error of at most 0.00045.
Values may be sent and summed in bfloat16 or wider, within the bound.
A program may use at most 64 MiB of HBM per device.

v0:
```python
import jax
import jax.numpy as jnp
from jax import lax
from jax.sharding import PartitionSpec as P

ITERS = 4


regularizer_epsilon = 0.05
highest = lax.Precision.HIGHEST


def row_total(part):
    return lax.psum(part, "tgt")


def col_total(part):
    return lax.psum(part, "src")


def times_vector(kernel, vector):
    return jnp.dot(kernel, vector, precision=highest, preferred_element_type=jnp.float32)


def vector_times(vector, kernel):
    return jnp.dot(vector, kernel, precision=highest, preferred_element_type=jnp.float32)


def per_device(src_emb, right_sentence_vectors, src_mass, tgt_mass):
    src_rows = lax.all_gather(src_emb, "tgt", axis=0, tiled=True)
    target_rows = lax.all_gather(right_sentence_vectors, "src", axis=0, tiled=True)

    def build():
        kernel_grid = (
            lax.dot_general(
                src_rows, target_rows, (((1,), (1,)), ((), ())), preferred_element_type=jnp.float32
            )
            / regularizer_epsilon
        )
        kernel = lax.optimization_barrier(jnp.exp(kernel_grid).astype(jnp.bfloat16))
        return (kernel_grid, kernel)

    kernel_grid, kernel = build()
    vector = jnp.ones(tgt_mass.shape, jnp.float32)
    old_saved, row_saved, src_saved, col_saved, tgt_saved = ([], [], [], [], [])
    for iteration in range(ITERS):
        old_saved.append(vector)
        row_sum = row_total(times_vector(kernel, vector))
        src_scale = src_mass / row_sum
        col_sum = col_total(vector_times(src_scale, kernel))
        vector = tgt_mass / col_sum
        row_saved.append(row_sum)
        src_saved.append(src_scale)
        col_saved.append(col_sum)
        tgt_saved.append(vector)
    last_src = src_saved[-1]
    last_tgt = tgt_saved[-1]
    weighted = kernel * kernel_grid
    src_adj = row_total(times_vector(weighted, last_tgt))
    tgt_adj = col_total(vector_times(last_src, weighted))
    row_bars = [None] * ITERS
    col_bars = [None] * ITERS
    for iteration in reversed(range(ITERS)):
        kernel_grid, kernel = build()
        col_bar = -tgt_adj * tgt_saved[iteration] / col_saved[iteration]
        back = row_total(times_vector(kernel, col_bar))
        if iteration == ITERS - 1:
            back = back + src_adj
        row_bar = -back * src_saved[iteration] / row_saved[iteration]
        if iteration > 0:
            tgt_adj = col_total(vector_times(row_bar, kernel))
        row_bars[iteration] = row_bar
        col_bars[iteration] = col_bar
    left = jnp.stack(row_bars + src_saved, axis=1)
    right = jnp.stack(old_saved + col_bars, axis=1)
    lowrank = lax.dot_general(
        left, right, (((1,), (1,)), ((), ())), precision=highest, preferred_element_type=jnp.float32
    )
    cross_term_grid = (
        kernel * (last_src[:, None] * last_tgt[None, :] * (1.0 + kernel_grid) + lowrank)
    ).astype(jnp.bfloat16)
    left_share_piece = (
        jnp.dot(cross_term_grid, target_rows, preferred_element_type=jnp.float32)
        / regularizer_epsilon
    )
    right_share_piece = (
        lax.dot_general(
            cross_term_grid, src_rows, (((0,), (0,)), ((), ())), preferred_element_type=jnp.float32
        )
        / regularizer_epsilon
    )
    src_whole = lax.psum(left_share_piece, "tgt")
    tgt_whole = lax.psum(right_share_piece, "src")
    src_count = src_emb.shape[0]
    tgt_count = right_sentence_vectors.shape[0]
    grad_src = lax.dynamic_slice_in_dim(src_whole, lax.axis_index("tgt") * src_count, src_count, 0)
    grad_tgt = lax.dynamic_slice_in_dim(tgt_whole, lax.axis_index("src") * tgt_count, tgt_count, 0)
    return (grad_src, grad_tgt)


def solution(mesh):
    placed = (P(("src", "tgt"), None), P(("tgt", "src"), None), P("src"), P("tgt"))
    return jax.shard_map(
        per_device,
        mesh=mesh,
        in_specs=placed,
        out_specs=(P(("src", "tgt"), None), P(("tgt", "src"), None)),
        check_vma=False,
    )
```

profile of v0, /device:TPU:0, one launch (start us, length us, event | category | flops | bytes accessed | tf_op | source)
XLA Modules:
  0.0 457.1 jit_solution(14965686141606025327)
XLA Ops:
  8.7 34.9 %all-gather.3.cloned.1.call-done = bf16[1024,768]{1,0:T(8,128)(2,1)} async-done(((bf16[256,768]{1,0:T(8,128)(2,1)}), bf16[1024,768]{1,0:T(8,128)(2,1)}) %all-gather.3.cloned.1.call-update) | async-done | bytes 1572880 | tf_op jit(solution)/shard_map/all_gather | solution.py:30
  43.5 26.7 %all-gather.5.cloned.1.call-done = bf16[1024,768]{1,0:T(8,128)(2,1)} async-done(((bf16[128,768]{1,0:T(8,128)(2,1)}), bf16[1024,768]{1,0:T(8,128)(2,1)}) %all-gather.5.cloned.1.call-update) | async-done | bytes 1572880 | tf_op jit(solution)/shard_map/all_gather | solution.py:31
  70.3 5.6 %exponential_convert_fusion = (bf16[1024,1024]{1,0:T(8,128)(2,1)S(1)}, f32[1024,1024]{1,0:T(8,128)}) fusion(bf16[1024,768]{1,0:T(8,128)(2,1)} %all-gather.3.cloned.1.call-done, bf16[1024,768]{1,0:T(8,128)(2,1)} %all-gather.5.cloned.1.call-done), kind=kOutput, calls=%fused_computation.3 | convolution fusion | flops 1612709888 | bytes 9437184 | tf_op jit(solution)/shard_map/dot_general | solution.py:35
  77.6 9.8 %psum.133 = f32[1024]{0:T(1024)S(1)} all-reduce(f32[1024]{0:T(1024)S(1)} %bitcast.122), channel_id=1, replica_groups=mesh['src'=8,'tgt'=4] {'tgt'}, use_global_device_ids=true, to_apply=%region_0.0 | all-reduce | flops 1024 | bytes 8192 | tf_op jit(solution)/shard_map/psum | solution.py:14
  88.4 13.6 %psum.134 = f32[1024]{0:T(1024)S(1)} all-reduce(f32[1024]{0:T(1024)S(1)} %bitcast.123), channel_id=1, replica_groups=mesh['src'=8,'tgt'=4] {'src'}, use_global_device_ids=true, to_apply=%region_1.0 | all-reduce | flops 1024 | bytes 8192 | tf_op jit(solution)/shard_map/psum | solution.py:18
  103.7 8.0 %psum.135 = f32[1024]{0:T(1024)S(1)} all-reduce(f32[1024]{0:T(1024)S(1)} %bitcast.124), channel_id=1, replica_groups=mesh['src'=8,'tgt'=4] {'tgt'}, use_global_device_ids=true, to_apply=%region_2.0 | all-reduce | flops 1024 | bytes 8192 | tf_op jit(solution)/shard_map/psum | solution.py:14
  112.6 13.6 %psum.136 = f32[1024]{0:T(1024)S(1)} all-reduce(f32[1024]{0:T(1024)S(1)} %bitcast.125), channel_id=1, replica_groups=mesh['src'=8,'tgt'=4] {'src'}, use_global_device_ids=true, to_apply=%region_3.0 | all-reduce | flops 1024 | bytes 8192 | tf_op jit(solution)/shard_map/psum | solution.py:18
  127.9 9.0 %psum.137 = f32[1024]{0:T(1024)S(1)} all-reduce(f32[1024]{0:T(1024)S(1)} %bitcast.126), channel_id=1, replica_groups=mesh['src'=8,'tgt'=4] {'tgt'}, use_global_device_ids=true, to_apply=%region_4.0 | all-reduce | flops 1024 | bytes 8192 | tf_op jit(solution)/shard_map/psum | solution.py:14
  137.8 13.6 %psum.138 = f32[1024]{0:T(1024)S(1)} all-reduce(f32[1024]{0:T(1024)S(1)} %bitcast.127), channel_id=1, replica_groups=mesh['src'=8,'tgt'=4] {'src'}, use_global_device_ids=true, to_apply=%region_5.0 | all-reduce | flops 1024 | bytes 8192 | tf_op jit(solution)/shard_map/psum | solution.py:18
  153.1 8.0 %psum.139 = f32[1024]{0:T(1024)S(1)} all-reduce(f32[1024]{0:T(1024)S(1)} %bitcast.128), channel_id=1, replica_groups=mesh['src'=8,'tgt'=4] {'tgt'}, use_global_device_ids=true, to_apply=%region_6.0 | all-reduce | flops 1024 | bytes 8192 | tf_op jit(solution)/shard_map/psum | solution.py:14
  162.0 4.6 %fusion.2 = f32[1,1024]{1,0:T(1,128)S(1)} fusion(f32[1024,1]{0,1:T(1,128)S(1)} %bitcast.88, bf16[1024,1024]{1,0:T(8,128)(2,1)S(1)} %get-tuple-element.6, f32[1024,1024]{1,0:T(8,128)} %get-tuple-element.7), kind=kOutput, calls=%fused_computation.5 | convolution fusion | flops 15728640 | bytes 6299648 | tf_op jit(solution)/shard_map/dot_general | solution.py:26
  166.7 13.9 %all-reduce = (f32[1024]{0:T(1024)S(1)}, f32[1024]{0:T(1024)S(1)}) all-reduce(f32[1024]{0:T(1024)S(1)} %bitcast.120, f32[1024]{0:T(1024)S(1)} %bitcast.121), channel_id=1, replica_groups=mesh['src'=8,'tgt'=4] {'src'}, use_global_device_ids=true, to_apply=%region_7.0 | all-reduce | flops 2048 | bytes 16384 | tf_op jit(solution)/shard_map/psum | solution.py:18
  180.6 6.1 %fusion.1 = f32[1,1024]{1,0:T(1,128)S(1)} fusion(f32[1024,1]{0,1:T(1,128)S(1)} %bitcast.102, bf16[1024,1024]{1,0:T(8,128)(2,1)S(1)} %get-tuple-element.6, f32[1024,1024]{1,0:T(8,128)} %get-tuple-element.7), kind=kOutput, calls=%fused_computation.4 | convolution fusion | flops 15728640 | bytes 6299648 | tf_op jit(solution)/shard_map/dot_general | solution.py:22
  188.5 9.8 %psum.152 = f32[1024]{0:T(1024)S(1)} all-reduce(f32[1024]{0:T(1024)S(1)} %add.58), channel_id=1, replica_groups=mesh['src'=8,'tgt'=4] {'tgt'}, use_global_device_ids=true, to_apply=%region_9.0 | all-reduce | flops 1024 | bytes 8192 | tf_op jit(solution)/shard_map/psum | solution.py:14
  199.2 13.6 %psum.144 = f32[1024]{0:T(1024)S(1)} all-reduce(f32[1024]{0:T(1024)S(1)} %bitcast.129), channel_id=1, replica_groups=mesh['src'=8,'tgt'=4] {'src'}, use_global_device_ids=true, to_apply=%region_11.0 | all-reduce | flops 1024 | bytes 8192 | tf_op jit(solution)/shard_map/psum | solution.py:18
  214.5 8.0 %psum.145 = f32[1024]{0:T(1024)S(1)} all-reduce(f32[1024]{0:T(1024)S(1)} %bitcast.130), channel_id=1, replica_groups=mesh['src'=8,'tgt'=4] {'tgt'}, use_global_device_ids=true, to_apply=%region_12.0 | all-reduce | flops 1024 | bytes 8192 | tf_op jit(solution)/shard_map/psum | solution.py:14
  223.4 13.6 %psum.146 = f32[1024]{0:T(1024)S(1)} all-reduce(f32[1024]{0:T(1024)S(1)} %bitcast.131), channel_id=1, replica_groups=mesh['src'=8,'tgt'=4] {'src'}, use_global_device_ids=true, to_apply=%region_13.0 | all-reduce | flops 1024 | bytes 8192 | tf_op jit(solution)/shard_map/psum | solution.py:18
  238.7 9.0 %psum.147 = f32[1024]{0:T(1024)S(1)} all-reduce(f32[1024]{0:T(1024)S(1)} %bitcast.132), channel_id=1, replica_groups=mesh['src'=8,'tgt'=4] {'tgt'}, use_global_device_ids=true, to_apply=%region_14.0 | all-reduce | flops 1024 | bytes 8192 | tf_op jit(solution)/shard_map/psum | solution.py:14
  248.6 13.6 %psum.148 = f32[1024]{0:T(1024)S(1)} all-reduce(f32[1024]{0:T(1024)S(1)} %bitcast.133), channel_id=1, replica_groups=mesh['src'=8,'tgt'=4] {'src'}, use_global_device_ids=true, to_apply=%region_15.0 | all-reduce | flops 1024 | bytes 8192 | tf_op jit(solution)/shard_map/psum | solution.py:18
  264.0 8.0 %psum.149 = f32[1024]{0:T(1024)S(1)} all-reduce(f32[1024]{0:T(1024)S(1)} %bitcast.119), channel_id=1, replica_groups=mesh['src'=8,'tgt'=4] {'tgt'}, use_global_device_ids=true, to_apply=%region_16.0 | all-reduce | flops 1024 | bytes 8192 | tf_op jit(solution)/shard_map/psum | solution.py:14
  272.1 6.2 %fusion = bf16[1024,1024]{1,0:T(8,128)(2,1)S(1)} fusion(bf16[1024,1024]{1,0:T(8,128)(2,1)S(1)} %get-tuple-element.6, f32[1024,1024]{1,0:T(8,128)} %get-tuple-element.7, f32[1024,8]{0,1:T(8,128)S(1)} %stack.56, f32[1024,8]{0,1:T(8,128)S(1)} %stack.64, f32[1024]{0:T(1024)S(1)} %get-tuple-element.5, f32[1024]{0:T(1024)S(1)} %div.68), kind=kOutput, calls=%fused_computation.2 | convolution fusion | flops 109051904 | bytes 8462336 | tf_op jit(solution)/shard_map/dot_general | solution.py:76
  284.9 4.9 %convolution_multiply_fusion.1 = f32[1024,768]{1,0:T(8,128)} fusion(bf16[1024,1024]{1,0:T(8,128)(2,1)S(1)} %copy-done.1, bf16[1024,768]{1,0:T(8,128)(2,1)} %all-gather.5.cloned.1.call-done), kind=kOutput, calls=%fused_computation.9 | convolution fusion | flops 1611399168 | bytes 6815744 | tf_op jit(solution)/shard_map/dot_general | solution.py:83
  289.8 68.7 %all-reduce.6.cloned.1.call-done = f32[1024,768]{1,0:T(8,128)} async-done(((f32[1024,768]{1,0:T(8,128)}), f32[1024,768]{1,0:T(8,128)}) %all-reduce.6.cloned.1.call-update) | async-done | bytes 3145744 | tf_op jit(solution)/shard_map/psum | solution.py:93
  360.2 88.3 %all-reduce.4.cloned.1.call-done = f32[1024,768]{1,0:T(8,128)} async-done(((f32[1024,768]{1,0:T(8,128)}), f32[1024,768]{1,0:T(8,128)}) %all-reduce.4.cloned.1.call-update) | async-done | bytes 3145744 | tf_op jit(solution)/shard_map/psum | solution.py:92
  (55 shorter events, 32.4 us)
Async XLA Ops:
  7.2 36.4 %all-gather.3.cloned.1.call-start = ((), (), s32[]{:S(2)}) async-start(), calls=%async_computation | async-start | bytes 1966080 | tf_op jit(solution)/shard_map/all_gather | solution.py:30
  7.9 62.4 %all-gather.5.cloned.1.call-start = ((), (), s32[]{:S(2)}) async-start(), calls=%async_computation.1 | async-start | bytes 1769472 | tf_op jit(solution)/shard_map/all_gather | solution.py:31
  8.6 349.8 %all-reduce.6.cloned.1.call-start = ((), (), s32[]{:S(2)}) async-start(), calls=%async_computation.3 | async-start | bytes 6291456 | tf_op jit(solution)/shard_map/psum | solution.py:93
  75.9 11.6 %copy-start.2 = (f32[1024]{0:T(1024)S(1)}, f32[1024]{0:T(1024)}, u32[]{:S(2)}) copy-start(f32[1024]{0:T(1024)} %param.6) | copy-start | bytes 12292
  75.9 26.1 %copy-start.3 = (f32[1024]{0:T(1024)S(1)}, f32[1024]{0:T(1024)}, u32[]{:S(2)}) copy-start(f32[1024]{0:T(1024)} %param.7) | copy-start | bytes 12292
  272.1 7.6 %copy-start.4 = (bf16[1024,768]{1,0:T(8,128)(2,1)S(1)}, bf16[1024,768]{1,0:T(8,128)(2,1)}, u32[]{:S(2)}) copy-start(bf16[1024,768]{1,0:T(8,128)(2,1)} %all-gather.3.cloned.1.call-done) | copy-start | bytes 4718596
  278.3 1.3 copy-start
  283.3 1.6 copy-start.1
  283.3 165.2 %all-reduce.4.cloned.1.call-start = ((), (), s32[]{:S(2)}) async-start(), calls=%async_computation.2 | async-start | bytes 6291456 | tf_op jit(solution)/shard_map/psum | solution.py:92
Sparse Core Ops, SparseCore 0:
  9.8 33.6 all-gather.2
  45.2 25.0 all-gather.4
  283.4 75.0 all-reduce.5
  361.4 87.0 all-reduce.3
where the time goes:
time: 458 us; the launch traced here: 457 us
  waiting for transfers between devices  220 us (48%)
  blocking collectives  165 us (36%)
  matrix products  51.4 us (11%)
  between operations  13.9 us (3%)
  local copies, waits for them, and re-layouts  6.84 us (1%)
    psum x7, blocking collectives, col_total(): return lax.psum(part, 'src')  95.4 us
    psum x1, waiting for transfers between devices, per_device(): src_whole = lax.psum(left_share_piece, 'tgt')  88.3 us
    psum x8, blocking collectives, row_total(): return lax.psum(part, 'tgt')  69.4 us
    psum x1, waiting for transfers between devices, per_device(): tgt_whole = lax.psum(right_share_piece, 'src')  68.7 us
    all_gather x1, waiting for transfers between devices, per_device(): src_rows = lax.all_gather(src_emb, 'tgt', axis=0, tiled=True)  34.9 us
    all_gather x1, waiting for transfers between devices, per_device(): lax.all_gather(right_sentence_vectors, 'src', axis=0, tiled=True)  26.7 us
    dot_general x9, matrix products, times_vector(): jnp.dot(kernel, vector, precision=highest, preferred_element_type=jnp.flo...  19.9 us
    dot_general x8, matrix products, vector_times(): jnp.dot(vector, kernel, precision=highest, preferred_element_type=jnp.flo...  11.1 us
  transfers between devices with their start and end apart: 4, of which 4 were waited for; matrix products, arithmetic and copies ran while one was open for 1% of the time, Pallas kernels for 0%

commit v1 on v0

v1 whole, which is shorter than its diff:
```python
import functools
import jax
import jax.numpy as jnp
from jax import lax
from jax.experimental import pallas as pl
from jax.experimental.pallas import tpu as pltpu
from jax.sharding import PartitionSpec as P

ITERS = 4
SCALE = 20.0
F32 = jnp.float32
BF16 = jnp.bfloat16
NN = (((1,), (0,)), ((), ()))
NT = (((1,), (1,)), ((), ()))
TN = (((0,), (0,)), ((), ()))
MESH = pl.DeviceIdType.MESH


def dot(a, b, dims):
    return lax.dot_general(a, b, dims, preferred_element_type=F32)


def split3(x):
    hi = x.astype(BF16).astype(F32)
    rest = x - hi
    mid = rest.astype(BF16).astype(F32)
    low = (rest - mid).astype(BF16).astype(F32)
    return hi, mid, low


def three_rows(x):
    hi, mid, low = split3(x)
    shape = (16, x.shape[1])
    row = lax.broadcasted_iota(jnp.int32, shape, 0)
    full = [jnp.broadcast_to(p, shape) for p in (hi, mid, low)]
    zero = jnp.zeros(shape, F32)
    return jnp.where(
        row == 0, full[0], jnp.where(row == 1, full[1], jnp.where(row == 2, full[2], zero))
    ).astype(BF16)


def body(
    ns, nt, src_ref, tgt_ref, smass_ref, tmass_ref, out_s, out_t,
    sr, tr, aff, ker, w1, w2, mix, lpart, rpair, rpart, lgot, rcore, rgot,
    ru, vc, rsum, csum, rbuf, cbuf, cbuf4,
    gs_send, gs_recv, gt_send, gt_recv, gc_send, gc_recv,
    r_send, r_recv, c_send, c_recv, c4_send, c4_recv,
    l_send, l_recv, x_send, x_recv, z_send, z_recv,
):
    me_t = lax.axis_index("tgt")
    me_s = lax.axis_index("src")
    nz = ns // 2
    core = lax.rem(me_s, 2)
    me_z = lax.div(me_s, 2)
    other = me_z * 2 + (1 - core)
    bs, d = src_ref.shape
    bt = tgt_ref.shape[0]
    rows, cols = nt * bs, ns * bt

    def peer_t(k):
        return lax.rem(me_t + k, nt)

    def peer_s(k):
        return lax.rem(me_s + k, ns)

    def peer_z(k):
        return lax.rem(me_z + k, nz)

    barrier = pltpu.get_barrier_semaphore()
    for k in range(1, nt):
        pl.semaphore_signal(barrier, inc=1, device_id=(me_s, peer_t(k)), device_id_type=MESH)
    for k in range(1, ns):
        pl.semaphore_signal(barrier, inc=1, device_id=(peer_s(k), me_t), device_id_type=MESH)
    pl.semaphore_wait(barrier, nt + ns - 2)

    def send(src, dst, s_sem, r_sem, dev):
        return pltpu.make_async_remote_copy(
            src_ref=src, dst_ref=dst, send_sem=s_sem, recv_sem=r_sem,
            device_id=dev, device_id_type=MESH,
        )

    gz = [
        send(tgt_ref, tr.at[me_s], gt_send.at[k], gt_recv.at[k], (peer_z(k) * 2 + core, me_t))
        for k in range(1, nz)
    ]
    gt = [
        send(src_ref, sr.at[me_t], gs_send.at[k], gs_recv.at[k], (me_s, peer_t(k)))
        for k in range(1, nt)
    ]
    for c in gz + gt:
        c.start()
    fwd = [send(tgt_ref, tr.at[me_s], gc_send.at[0], gc_recv.at[0], (other, me_t))]
    fwd[0].start()
    sr[me_t] = src_ref[...]
    tr[me_s] = tgt_ref[...]
    for k in range(1, nz):
        gz[k - 1].wait_recv()
        blk = lax.rem(me_z + nz - k, nz) * 2 + core
        c = send(tr.at[blk], tr.at[blk], gc_send.at[k], gc_recv.at[k], (other, me_t))
        c.start()
        fwd.append(c)
    for c in gt + fwd:
        c.wait()
    for c in gz:
        c.wait_send()

    def build(i, carry):
        a = dot(sr[i], tr[...].reshape(cols, d), NT) * SCALE
        kb = jnp.exp(a).astype(BF16)
        ker[i] = kb
        aff[i] = a
        w = kb.astype(F32) * a
        h = w.astype(BF16)
        w1[i] = h
        w2[i] = (w - h.astype(F32)).astype(BF16)
        return carry

    lax.fori_loop(0, nt, build, 0)

    def row_pass(m, x):
        return jnp.sum(dot(three_rows(x), m[...].reshape(rows, cols), NT), axis=0, keepdims=True)

    def col_pass(m, x):
        return jnp.sum(dot(three_rows(x), m[...].reshape(rows, cols), NN), axis=0, keepdims=True)

    def row_total(step, part):
        rbuf[step, me_t] = part
        cs = [
            send(rbuf.at[step, me_t], rbuf.at[step, me_t], r_send.at[step, k], r_recv.at[step, k],
                 (me_s, peer_t(k)))
            for k in range(1, nt)
        ]
        for c in cs:
            c.start()
        for c in cs:
            c.wait()
        total = rbuf[step, 0]
        for i in range(1, nt):
            total = total + rbuf[step, i]
        return total

    def col_start(buf, send_sem, recv_sem):
        cs = [
            send(buf.at[me_s], buf.at[me_s], send_sem.at[k], recv_sem.at[k], (peer_s(k), me_t))
            for k in range(1, ns)
        ]
        for c in cs:
            c.start()
        for c in cs:
            c.wait()
        total = buf[0]
        for i in range(1, ns):
            total = total + buf[i]
        return total

    def col_total(step, part):
        cbuf[step, me_s] = part
        return col_start(cbuf.at[step], c_send.at[step], c_recv.at[step])

    vc[pl.ds(0, 1), :] = jnp.ones((1, cols), F32)

    def scale_src(k):
        r = row_total(k, row_pass(ker, vc[pl.ds(k, 1), :]))
        u = smass_ref[...] / r
        rsum[pl.ds(k, 1), :] = r
        ru[pl.ds(ITERS + k, 1), :] = u
        return u

    def forward(k, carry):
        u = scale_src(k)
        c = col_total(k, col_pass(ker, u))
        csum[pl.ds(k, 1), :] = c
        vc[pl.ds(k + 1, 1), :] = tmass_ref[...] / c
        return carry

    lax.fori_loop(0, ITERS - 1, forward, 0)
    last = ITERS - 1
    u4 = scale_src(last)
    cbuf4[me_s, :, pl.ds(0, cols)] = col_pass(ker, u4)
    cbuf4[me_s, :, pl.ds(cols, cols)] = col_pass(w1, u4) + col_pass(w2, u4)
    both = col_start(cbuf4, c4_send, c4_recv)
    c4, tgt_adj = both[:, :cols], both[:, cols:]
    v4 = tmass_ref[...] / c4
    cbar = -tgt_adj * v4 / c4
    vc[pl.ds(ITERS + last, 1), :] = cbar
    part = row_pass(ker, cbar) + (row_pass(w1, v4) + row_pass(w2, v4))

    def rbar_of(k, part):
        back = row_total(ITERS + k, part)
        rbar = -back * ru[pl.ds(ITERS + k, 1), :] / rsum[pl.ds(k, 1), :]
        ru[pl.ds(k, 1), :] = rbar
        return rbar

    rbar = rbar_of(last, part)

    def backward(j, rbar):
        k = last - 1 - j
        adj = col_total(last + j, col_pass(ker, rbar))
        cbar = -adj * vc[pl.ds(k + 1, 1), :] / csum[pl.ds(k, 1), :]
        vc[pl.ds(ITERS + k, 1), :] = cbar
        return rbar_of(k, row_pass(ker, cbar))

    lax.fori_loop(0, ITERS - 1, backward, rbar)

    lh, lm, ll = split3(ru[...])
    rh, rm, rl = split3(vc[...])
    zero = jnp.zeros((8, cols), F32)
    lstack = jnp.concatenate(
        [lh, lh, lm, lm, lh, ll, jnp.broadcast_to(u4, (8, rows)), jnp.zeros((8, rows), F32)], axis=0
    )
    lcol = lstack.T
    rstack = jnp.concatenate([rh, rm, rh, rm, rl, rh, zero, zero], axis=0).astype(BF16)
    for i in range(nt):
        blk = lcol[i * bs:(i + 1) * bs]
        lk = blk.astype(BF16)
        low = dot(lk, rstack, NN)
        ucol = blk[:, 48:49]
        m = ker[i].astype(F32) * (ucol * v4 * (1.0 + aff[i]) + low)
        mix[i] = m.astype(BF16)

    lcopies = []
    for k in list(range(1, nt)):
        i = peer_t(k)
        lpart[k] = dot(mix[i], tr[...].reshape(cols, d), NN) * SCALE
        c = send(lpart.at[k], lgot.at[k], l_send.at[k], l_recv.at[k], (me_s, i))
        c.start()
        lcopies.append(c)

    xcopies = []
    for k in range(nz):
        z = peer_z(k + 1)
        m = mix[:, :, pl.ds(pl.multiple_of(z * (2 * bt), 2 * bt), 2 * bt)].reshape(rows, 2 * bt)
        pair = dot(m, sr[...].reshape(rows, d), TN) * SCALE
        rpair[k] = pair.reshape(2, bt, d)
        c = send(rpair.at[k, 1 - core], rcore.at[k], x_send.at[k], x_recv.at[k], (other, me_t))
        c.start()
        xcopies.append(c)
    zcopies = []
    for k in range(nz):
        z = peer_z(k + 1)
        xcopies[k].wait()
        rpart[k] = rpair[k, core] + rcore[k]
        if k < nz - 1:
            c = send(rpart.at[k], rgot.at[k], z_send.at[k], z_recv.at[k], (z * 2 + core, me_t))
            c.start()
            zcopies.append(c)
    total = dot(mix[me_t], tr[...].reshape(cols, d), NN) * SCALE
    for k in range(1, nt):
        lcopies[k - 1].wait()
        total = total + lgot[k]
    out_s[...] = total
    total = rpart[nz - 1]
    for k in range(nz - 1):
        zcopies[k].wait()
        total = total + rgot[k]
    out_t[...] = total


def per_device(ns, nt, src_emb, right_sentence_vectors, src_mass, tgt_mass):
    bs, d = src_emb.shape
    bt = right_sentence_vectors.shape[0]
    rows, cols = nt * bs, ns * bt
    nz = ns // 2
    dma = pltpu.SemaphoreType.DMA
    v = pltpu.VMEM
    scratch = [
        v((nt, bs, d), BF16), v((ns, bt, d), BF16),
        v((nt, bs, cols), F32), v((nt, bs, cols), BF16), v((nt, bs, cols), BF16),
        v((nt, bs, cols), BF16), v((nt, bs, cols), BF16),
        v((nt, bs, d), F32), v((nz, 2, bt, d), F32), v((nz, bt, d), F32), v((nt, bs, d), F32),
        v((nz, bt, d), F32), v((nz, bt, d), F32),
        v((2 * ITERS, rows), F32), v((2 * ITERS, cols), F32), v((8, rows), F32), v((8, cols), F32),
        v((2 * ITERS, nt, 1, rows), F32), v((2 * ITERS - 2, ns, 1, cols), F32),
        v((ns, 1, 2 * cols), F32),
        dma((nt,)), dma((nt,)), dma((nz,)), dma((nz,)), dma((nz,)), dma((nz,)),
        dma((2 * ITERS, nt)), dma((2 * ITERS, nt)),
        dma((2 * ITERS - 2, ns)), dma((2 * ITERS - 2, ns)), dma((ns,)), dma((ns,)),
        dma((nt,)), dma((nt,)), dma((nz,)), dma((nz,)), dma((nz,)), dma((nz,)),
    ]
    vm = pl.BlockSpec(memory_space=pltpu.VMEM)
    return pl.pallas_call(
        functools.partial(body, ns, nt),
        out_shape=(jax.ShapeDtypeStruct((bs, d), F32), jax.ShapeDtypeStruct((bt, d), F32)),
        in_specs=[vm] * 4,
        out_specs=(vm, vm),
        scratch_shapes=scratch,
        compiler_params=pltpu.CompilerParams(
            collective_id=0, has_side_effects=True, vmem_limit_bytes=50 * 1024 * 1024
        ),
    )(src_emb, right_sentence_vectors, src_mass.reshape(1, rows), tgt_mass.reshape(1, cols))


def solution(mesh):
    ns, nt = mesh.shape["src"], mesh.shape["tgt"]
    placed = (P(("src", "tgt"), None), P(("tgt", "src"), None), P("src"), P("tgt"))
    return jax.shard_map(
        functools.partial(per_device, ns, nt),
        mesh=mesh,
        in_specs=placed,
        out_specs=(P(("src", "tgt"), None), P(("tgt", "src"), None)),
        check_vma=False,
    )
```

time: 458 us -> 135 us (0.29)
  waiting for transfers between devices: 220 us -> 0 us
  blocking collectives: 165 us -> 0 us
  Pallas kernels: 0 us -> 128 us
  matrix products: 51.4 us -> 0 us
  between operations: 13.9 us -> 0.65 us
    psum x15 -> x0, blocking collectives: 165 us -> none  [the longest x7 95.4 us: col_total(): return lax.psum(part, 'src')]
    psum x2 -> x0, waiting for transfers between devices: 157 us -> none  [the longest x1 88.3 us: per_device(): src_whole = lax.psum(left_share_piece, 'tgt')]
    pallas_call x0 -> x1, Pallas kernels: none -> 128 us  [per_device(): pl.pallas_call(functools.partial(body, ns, nt), out_shape=(jax.ShapeDtype...]
    all_gather x2 -> x0, waiting for transfers between devices: 61.6 us -> none  [the longest x1 34.9 us: per_device(): src_rows = lax.all_gather(src_emb, 'tgt', axis=0, tiled=True)]
    dot_general x21 -> x0, matrix products: 51.4 us -> none  [the longest x9 19.9 us: times_vector(): jnp.dot(kernel, vector, precision=highest, preferred_element_type=jnp.flo...]
  transfers between devices with their start and end apart: 4 -> 0, of which waited for: 4 -> 0; matrix products, arithmetic and copies ran while one was open for 1% -> 0% of each run, Pallas kernels for 0% -> 0%
where the time goes in v1:
time: 135 us; the launch traced here: 134 us
  Pallas kernels  128 us (95%)
  local copies, waits for them, and re-layouts  4.92 us (4%)
    pallas_call x1, Pallas kernels, per_device(): pl.pallas_call(functools.partial(body, ns, nt), out_shape=(jax.ShapeDtype...  128 us
    unnamed x10, local copies, waits for them, and re-layouts  4.92 us

profile of v1, /device:TPU:0, one launch (start us, length us, event | category | flops | bytes accessed | tf_op | source)
XLA Modules:
  0.0 133.9 jit_solution(15640881574347366735)
XLA Ops:
  0.6 0.0 copy-start
  0.6 1.0 copy-done
  1.6 0.0 copy-start.1
  1.6 0.9 copy-done.1
  2.6 0.0 copy-start.2
  2.6 0.7 copy-done.2
  3.2 0.0 copy-start.3
  3.2 0.7 copy-done.3
  3.9 128.4 %shard_map.59 = (f32[256,768]{1,0:T(8,128)S(1)}, f32[128,768]{1,0:T(8,128)S(1)}) custom-call(bf16[256,768]{1,0:T(8,128)(2,1)S(1)} %copy-done, bf16[128,768]{1,0:T(8,128)(2,1)S(1)} %copy-done.1, f32[1,1024]{1,0:T(1,128)S(1)} %bitcast.2, f32[1,1024]{1,0:T(1,128)S(1)} %bitcast.3), custom_call_target="tpu_custom_call" | custom-call | tf_op jit(solution)/shard_map/pallas_call | solution.py:281
  132.3 0.9 copy.8
  133.2 0.7 copy.9
Async XLA Ops:
  0.6 1.0 copy-start
  1.6 0.9 copy-start.1
  2.6 0.7 copy-start.2
  3.2 0.7 copy-start.3

commit v2 on v1

--- a/solution.py
+++ b/solution.py
@@ -8,6 +8,8 @@
 
 ITERS = 4
 SCALE = 20.0
+SPAN = 80.0
+TINY = 1e-30
 F32 = jnp.float32
 BF16 = jnp.bfloat16
 NN = (((1,), (0,)), ((), ()))
@@ -39,13 +41,23 @@
     ).astype(BF16)
 
 
+def encode(x):
+    m = jnp.maximum(jnp.max(jnp.abs(x), axis=0, keepdims=True), TINY)
+    return jnp.exp(x * (SPAN / m)).astype(BF16), m * (1.0 / SPAN)
+
+
+def decode(y, m):
+    return jnp.log(y.astype(F32)) * m
+
+
 def body(
-    ns, nt, src_ref, tgt_ref, smass_ref, tmass_ref, out_s, out_t,
-    sr, tr, aff, ker, w1, w2, mix, lpart, rpair, rpart, lgot, rcore, rgot,
-    ru, vc, rsum, csum, rbuf, cbuf, cbuf4,
+    ns, nt, src_ref, tgt_ref, smass_hbm, tmass_hbm, out_s, out_t, smass_ref, tmass_ref, own_sem,
+    sr, tr, aff, ker, w1, w2, mix, lpart, rpair, rpart, lgot, rcore, rgot, lscale, lsgot, rscale, rsgot,
+    ru, vc, rsum, csum, rbuf, cbuf,
     gs_send, gs_recv, gt_send, gt_recv, gc_send, gc_recv,
-    r_send, r_recv, c_send, c_recv, c4_send, c4_recv,
+    r_send, r_recv, c_send, c_recv,
     l_send, l_recv, x_send, x_recv, z_send, z_recv,
+    ls_send, ls_recv, zs_send, zs_recv,
 ):
     me_t = lax.axis_index("tgt")
     me_s = lax.axis_index("src")
@@ -79,6 +91,12 @@
             device_id=dev, device_id_type=MESH,
         )
 
+    own = [
+        pltpu.make_async_copy(src_ref, sr.at[me_t], own_sem.at[0]),
+        pltpu.make_async_copy(tgt_ref, tr.at[me_s], own_sem.at[1]),
+        pltpu.make_async_copy(smass_hbm, smass_ref, own_sem.at[2]),
+        pltpu.make_async_copy(tmass_hbm, tmass_ref, own_sem.at[3]),
+    ]
     gz = [
         send(tgt_ref, tr.at[me_s], gt_send.at[k], gt_recv.at[k], (peer_z(k) * 2 + core, me_t))
         for k in range(1, nz)
@@ -91,29 +109,32 @@
         c.start()
     fwd = [send(tgt_ref, tr.at[me_s], gc_send.at[0], gc_recv.at[0], (other, me_t))]
     fwd[0].start()
-    sr[me_t] = src_ref[...]
-    tr[me_s] = tgt_ref[...]
+    for c in own:
+        c.start()
     for k in range(1, nz):
         gz[k - 1].wait_recv()
         blk = lax.rem(me_z + nz - k, nz) * 2 + core
         c = send(tr.at[blk], tr.at[blk], gc_send.at[k], gc_recv.at[k], (other, me_t))
         c.start()
         fwd.append(c)
-    for c in gt + fwd:
+    for c in own + gt + fwd:
         c.wait()
     for c in gz:
         c.wait_send()
 
     def build(i, carry):
         a = dot(sr[i], tr[...].reshape(cols, d), NT) * SCALE
-        kb = jnp.exp(a).astype(BF16)
-        ker[i] = kb
+        ker[i] = jnp.exp(a).astype(BF16)
         aff[i] = a
-        w = kb.astype(F32) * a
-        h = w.astype(BF16)
-        w1[i] = h
-        w2[i] = (w - h.astype(F32)).astype(BF16)
         return carry
+
+    def weigh(k):
+        for j in range(nt // ITERS):
+            i = k * (nt // ITERS) + j
+            w = ker[i].astype(F32) * aff[i]
+            h = w.astype(BF16)
+            w1[i] = h
+            w2[i] = (w - h.astype(F32)).astype(BF16)
 
     lax.fori_loop(0, nt, build, 0)
 
@@ -123,7 +144,7 @@
     def col_pass(m, x):
         return jnp.sum(dot(three_rows(x), m[...].reshape(rows, cols), NN), axis=0, keepdims=True)
 
-    def row_total(step, part):
+    def row_total(step, part, during=None):
         rbuf[step, me_t] = part
         cs = [
             send(rbuf.at[step, me_t], rbuf.at[step, me_t], r_send.at[step, k], r_recv.at[step, k],
@@ -132,6 +153,8 @@
         ]
         for c in cs:
             c.start()
+        if during is not None:
+            during()
         for c in cs:
             c.wait()
         total = rbuf[step, 0]
@@ -139,28 +162,32 @@
             total = total + rbuf[step, i]
         return total
 
-    def col_start(buf, send_sem, recv_sem):
+    def col_start(step, part):
+        cbuf[step, me_s] = part
         cs = [
-            send(buf.at[me_s], buf.at[me_s], send_sem.at[k], recv_sem.at[k], (peer_s(k), me_t))
+            send(cbuf.at[step, me_s], cbuf.at[step, me_s], c_send.at[step, k], c_recv.at[step, k],
+                 (peer_s(k), me_t))
             for k in range(1, ns)
         ]
         for c in cs:
             c.start()
+        return cs
+
+    def col_done(step, cs):
         for c in cs:
             c.wait()
-        total = buf[0]
+        total = cbuf[step, 0]
         for i in range(1, ns):
-            total = total + buf[i]
+            total = total + cbuf[step, i]
         return total
 
     def col_total(step, part):
-        cbuf[step, me_s] = part
-        return col_start(cbuf.at[step], c_send.at[step], c_recv.at[step])
+        return col_done(step, col_start(step, part))
 
     vc[pl.ds(0, 1), :] = jnp.ones((1, cols), F32)
 
     def scale_src(k):
-        r = row_total(k, row_pass(ker, vc[pl.ds(k, 1), :]))
+        r = row_total(k, row_pass(ker, vc[pl.ds(k, 1), :]), lambda: weigh(k))
         u = smass_ref[...] / r
         rsum[pl.ds(k, 1), :] = r
         ru[pl.ds(ITERS + k, 1), :] = u
@@ -176,14 +203,15 @@
     lax.fori_loop(0, ITERS - 1, forward, 0)
     last = ITERS - 1
     u4 = scale_src(last)
-    cbuf4[me_s, :, pl.ds(0, cols)] = col_pass(ker, u4)
-    cbuf4[me_s, :, pl.ds(cols, cols)] = col_pass(w1, u4) + col_pass(w2, u4)
-    both = col_start(cbuf4, c4_send, c4_recv)
-    c4, tgt_adj = both[:, :cols], both[:, cols:]
+    first = col_start(last, col_pass(ker, u4))
+    second = col_start(2 * last + 1, col_pass(w1, u4) + col_pass(w2, u4))
+    c4 = col_done(last, first)
     v4 = tmass_ref[...] / c4
+    src_adj = row_pass(w1, v4) + row_pass(w2, v4)
+    tgt_adj = col_done(2 * last + 1, second)
     cbar = -tgt_adj * v4 / c4
     vc[pl.ds(ITERS + last, 1), :] = cbar
-    part = row_pass(ker, cbar) + (row_pass(w1, v4) + row_pass(w2, v4))
+    part = row_pass(ker, cbar) + src_adj
 
     def rbar_of(k, part):
         back = row_total(ITERS + k, part)
@@ -195,7 +223,7 @@
 
     def backward(j, rbar):
         k = last - 1 - j
-        adj = col_total(last + j, col_pass(ker, rbar))
+        adj = col_total(ITERS + j, col_pass(ker, rbar))
         cbar = -adj * vc[pl.ds(k + 1, 1), :] / csum[pl.ds(k, 1), :]
         vc[pl.ds(ITERS + k, 1), :] = cbar
         return rbar_of(k, row_pass(ker, cbar))
@@ -219,15 +247,18 @@
         mix[i] = m.astype(BF16)
 
     lcopies = []
-    for k in list(range(1, nt)):
+    xcopies = []
+    zcopies = []
+
+    def left(k):
         i = peer_t(k)
-        lpart[k] = dot(mix[i], tr[...].reshape(cols, d), NN) * SCALE
-        c = send(lpart.at[k], lgot.at[k], l_send.at[k], l_recv.at[k], (me_s, i))
-        c.start()
-        lcopies.append(c)
-
-    xcopies = []
-    for k in range(nz):
+        lpart[k], lscale[k] = encode(dot(mix[i], tr[...].reshape(cols, d), NN) * SCALE)
+        lcopies.append(send(lpart.at[k], lgot.at[k], l_send.at[k], l_recv.at[k], (me_s, i)))
+        lcopies.append(send(lscale.at[k], lsgot.at[k], ls_send.at[k], ls_recv.at[k], (me_s, i)))
+        lcopies[-2].start()
+        lcopies[-1].start()
+
+    def right(k):
         z = peer_z(k + 1)
         m = mix[:, :, pl.ds(pl.multiple_of(z * (2 * bt), 2 * bt), 2 * bt)].reshape(rows, 2 * bt)
         pair = dot(m, sr[...].reshape(rows, d), TN) * SCALE
@@ -235,24 +266,38 @@
         c = send(rpair.at[k, 1 - core], rcore.at[k], x_send.at[k], x_recv.at[k], (other, me_t))
         c.start()
         xcopies.append(c)
-    zcopies = []
-    for k in range(nz):
+
+    def along_z(k):
         z = peer_z(k + 1)
         xcopies[k].wait()
-        rpart[k] = rpair[k, core] + rcore[k]
-        if k < nz - 1:
-            c = send(rpart.at[k], rgot.at[k], z_send.at[k], z_recv.at[k], (z * 2 + core, me_t))
-            c.start()
-            zcopies.append(c)
+        rpart[k], rscale[k] = encode(rpair[k, core] + rcore[k])
+        dev = (z * 2 + core, me_t)
+        zcopies.append(send(rpart.at[k], rgot.at[k], z_send.at[k], z_recv.at[k], dev))
+        zcopies.append(send(rscale.at[k], rsgot.at[k], zs_send.at[k], zs_recv.at[k], dev))
+        zcopies[-2].start()
+        zcopies[-1].start()
+
+    right(0)
+    left(1)
+    for k in range(1, nz):
+        right(k)
+        along_z(k - 1)
+        if k + 1 < nt:
+            left(k + 1)
+    for k in range(nz + 1, nt):
+        left(k)
     total = dot(mix[me_t], tr[...].reshape(cols, d), NN) * SCALE
     for k in range(1, nt):
-        lcopies[k - 1].wait()
-        total = total + lgot[k]
+        lcopies[2 * k - 2].wait()
+        lcopies[2 * k - 1].wait()
+        total = total + decode(lgot[k], lsgot[k])
     out_s[...] = total
-    total = rpart[nz - 1]
+    xcopies[nz - 1].wait()
+    total = rpair[nz - 1, core] + rcore[nz - 1]
     for k in range(nz - 1):
-        zcopies[k].wait()
-        total = total + rgot[k]
+        zcopies[2 * k].wait()
+        zcopies[2 * k + 1].wait()
+        total = total + decode(rgot[k], rsgot[k])
     out_t[...] = total
 
 
@@ -264,24 +309,26 @@
     dma = pltpu.SemaphoreType.DMA
     v = pltpu.VMEM
     scratch = [
+        v((1, rows), F32), v((1, cols), F32), dma((4,)),
         v((nt, bs, d), BF16), v((ns, bt, d), BF16),
         v((nt, bs, cols), F32), v((nt, bs, cols), BF16), v((nt, bs, cols), BF16),
         v((nt, bs, cols), BF16), v((nt, bs, cols), BF16),
-        v((nt, bs, d), F32), v((nz, 2, bt, d), F32), v((nz, bt, d), F32), v((nt, bs, d), F32),
-        v((nz, bt, d), F32), v((nz, bt, d), F32),
+        v((nt, bs, d), BF16), v((nz, 2, bt, d), F32), v((nz, bt, d), BF16), v((nt, bs, d), BF16),
+        v((nz, bt, d), F32), v((nz, bt, d), BF16),
+        v((nt, 1, d), F32), v((nt, 1, d), F32), v((nz, 1, d), F32), v((nz, 1, d), F32),
         v((2 * ITERS, rows), F32), v((2 * ITERS, cols), F32), v((8, rows), F32), v((8, cols), F32),
-        v((2 * ITERS, nt, 1, rows), F32), v((2 * ITERS - 2, ns, 1, cols), F32),
-        v((ns, 1, 2 * cols), F32),
+        v((2 * ITERS, nt, 1, rows), F32), v((2 * ITERS, ns, 1, cols), F32),
         dma((nt,)), dma((nt,)), dma((nz,)), dma((nz,)), dma((nz,)), dma((nz,)),
         dma((2 * ITERS, nt)), dma((2 * ITERS, nt)),
-        dma((2 * ITERS - 2, ns)), dma((2 * ITERS - 2, ns)), dma((ns,)), dma((ns,)),
+        dma((2 * ITERS, ns)), dma((2 * ITERS, ns)),
         dma((nt,)), dma((nt,)), dma((nz,)), dma((nz,)), dma((nz,)), dma((nz,)),
+        dma((nt,)), dma((nt,)), dma((nz,)), dma((nz,)),
     ]
     vm = pl.BlockSpec(memory_space=pltpu.VMEM)
     return pl.pallas_call(
         functools.partial(body, ns, nt),
         out_shape=(jax.ShapeDtypeStruct((bs, d), F32), jax.ShapeDtypeStruct((bt, d), F32)),
-        in_specs=[vm] * 4,
+        in_specs=[pl.BlockSpec(memory_space=pl.ANY)] * 4,
         out_specs=(vm, vm),
         scratch_shapes=scratch,
         compiler_params=pltpu.CompilerParams(

time: 135 us -> 118 us (0.87)
  Pallas kernels: 128 us -> 112 us
    pallas_call x1, Pallas kernels: 128 us -> 112 us  [per_device(): pl.pallas_call(functools.partial(body, ns, nt), out_shape=(jax.ShapeDtype...]
where the time goes in v2:
time: 118 us
  Pallas kernels  112 us (95%)
  local copies, waits for them, and re-layouts  4.92 us (4%)
    pallas_call x1, Pallas kernels, per_device(): pl.pallas_call(functools.partial(body, ns, nt), out_shape=(jax.ShapeDtype...  112 us
    unnamed x10, local copies, waits for them, and re-layouts  4.92 us

profile of v2, /device:TPU:0, one launch (start us, length us, event | category | flops | bytes accessed | tf_op | source)
XLA Modules:
  0.0 117.9 jit_solution(9046864177334378730)
XLA Ops:
  0.6 0.0 copy-start
  0.6 1.0 copy-done
  1.6 0.0 copy-start.1
  1.6 0.9 copy-done.1
  2.6 0.0 copy-start.2
  2.6 0.7 copy-done.2
  3.2 0.0 copy-start.3
  3.2 0.7 copy-done.3
  3.9 112.4 %shard_map.59 = (f32[256,768]{1,0:T(8,128)S(1)}, f32[128,768]{1,0:T(8,128)S(1)}) custom-call(bf16[256,768]{1,0:T(8,128)(2,1)S(1)} %copy-done, bf16[128,768]{1,0:T(8,128)(2,1)S(1)} %copy-done.1, f32[1,1024]{1,0:T(1,128)S(1)} %bitcast.2, f32[1,1024]{1,0:T(1,128)S(1)} %bitcast.3), custom_call_target="tpu_custom_call" | custom-call | tf_op jit(solution)/shard_map/pallas_call | solution.py:328
  116.3 0.9 copy.8
  117.2 0.7 copy.9
Async XLA Ops:
  0.6 1.0 copy-start
  1.6 0.9 copy-start.1
  2.6 0.7 copy-start.2
  3.2 0.7 copy-start.3

commit v3 on v2

--- a/solution.py
+++ b/solution.py
@@ -105,7 +105,7 @@
         send(src_ref, sr.at[me_t], gs_send.at[k], gs_recv.at[k], (me_s, peer_t(k)))
         for k in range(1, nt)
     ]
-    for c in gz + gt:
+    for c in gz + gt[::-1]:
         c.start()
     fwd = [send(tgt_ref, tr.at[me_s], gc_send.at[0], gc_recv.at[0], (other, me_t))]
     fwd[0].start()
@@ -117,16 +117,26 @@
         c = send(tr.at[blk], tr.at[blk], gc_send.at[k], gc_recv.at[k], (other, me_t))
         c.start()
         fwd.append(c)
-    for c in own + gt + fwd:
+    for c in own + gt:
         c.wait()
     for c in gz:
         c.wait_send()
 
-    def build(i, carry):
-        a = dot(sr[i], tr[...].reshape(cols, d), NT) * SCALE
-        ker[i] = jnp.exp(a).astype(BF16)
-        aff[i] = a
-        return carry
+    def build(z):
+        at = pl.ds(pl.multiple_of(z * (2 * bt), 2 * bt), 2 * bt)
+        pair = tr[pl.ds(2 * z, 2)].reshape(2 * bt, d)
+
+        def rows_of(i, carry):
+            a = dot(sr[i], pair, NT) * SCALE
+            ker[i, :, at] = jnp.exp(a).astype(BF16)
+            aff[i, :, at] = a
+            return carry
+
+        lax.fori_loop(0, nt, rows_of, 0, unroll=True)
+
+    for k in range(nz):
+        fwd[k].wait()
+        build(lax.rem(me_z + nz - k, nz))
 
     def weigh(k):
         for j in range(nt // ITERS):
@@ -136,7 +146,6 @@
             w1[i] = h
             w2[i] = (w - h.astype(F32)).astype(BF16)
 
-    lax.fori_loop(0, nt, build, 0)
 
     def row_pass(m, x):
         return jnp.sum(dot(three_rows(x), m[...].reshape(rows, cols), NT), axis=0, keepdims=True)
@@ -213,8 +222,8 @@
     vc[pl.ds(ITERS + last, 1), :] = cbar
     part = row_pass(ker, cbar) + src_adj
 
-    def rbar_of(k, part):
-        back = row_total(ITERS + k, part)
+    def rbar_of(k, part, during=None):
+        back = row_total(ITERS + k, part, during)
         rbar = -back * ru[pl.ds(ITERS + k, 1), :] / rsum[pl.ds(k, 1), :]
         ru[pl.ds(k, 1), :] = rbar
         return rbar
@@ -228,35 +237,46 @@
         vc[pl.ds(ITERS + k, 1), :] = cbar
         return rbar_of(k, row_pass(ker, cbar))
 
-    lax.fori_loop(0, ITERS - 1, backward, rbar)
-
-    lh, lm, ll = split3(ru[...])
-    rh, rm, rl = split3(vc[...])
-    zero = jnp.zeros((8, cols), F32)
-    lstack = jnp.concatenate(
-        [lh, lh, lm, lm, lh, ll, jnp.broadcast_to(u4, (8, rows)), jnp.zeros((8, rows), F32)], axis=0
-    )
-    lcol = lstack.T
-    rstack = jnp.concatenate([rh, rm, rh, rm, rl, rh, zero, zero], axis=0).astype(BF16)
+    rbar = lax.fori_loop(0, ITERS - 2, backward, rbar)
+    ru[pl.ds(0, 1), :] = jnp.zeros((1, rows), F32)
+    adj = col_total(ITERS + last - 1, col_pass(ker, rbar))
+    cbar = -adj * vc[pl.ds(1, 1), :] / csum[pl.ds(0, 1), :]
+    vc[pl.ds(ITERS, 1), :] = cbar
+
+    def base():
+        lh, lm, ll = split3(ru[...])
+        rh, rm, rl = split3(vc[...])
+        zero = jnp.zeros((8, cols), F32)
+        lstack = jnp.concatenate(
+            [lh, lh, lm, lm, lh, ll, jnp.broadcast_to(u4, (8, rows)), jnp.zeros((8, rows), F32)],
+            axis=0,
+        )
+        lcol = lstack.T
+        rstack = jnp.concatenate([rh, rm, rh, rm, rl, rh, zero, zero], axis=0).astype(BF16)
+        for i in range(nt):
+            blk = lcol[i * bs:(i + 1) * bs]
+            low = dot(blk.astype(BF16), rstack, NN)
+            aff[i] = blk[:, 48:49] * v4 * (1.0 + aff[i]) + low
+
+    rbar = rbar_of(0, row_pass(ker, cbar), base)
+    rcol = jnp.broadcast_to(rbar, (8, rows)).T
     for i in range(nt):
-        blk = lcol[i * bs:(i + 1) * bs]
-        lk = blk.astype(BF16)
-        low = dot(lk, rstack, NN)
-        ucol = blk[:, 48:49]
-        m = ker[i].astype(F32) * (ucol * v4 * (1.0 + aff[i]) + low)
+        m = ker[i].astype(F32) * (aff[i] + rcol[i * bs:(i + 1) * bs, 0:1])
         mix[i] = m.astype(BF16)
 
-    lcopies = []
+    lcopies = {}
     xcopies = []
     zcopies = []
 
     def left(k):
         i = peer_t(k)
         lpart[k], lscale[k] = encode(dot(mix[i], tr[...].reshape(cols, d), NN) * SCALE)
-        lcopies.append(send(lpart.at[k], lgot.at[k], l_send.at[k], l_recv.at[k], (me_s, i)))
-        lcopies.append(send(lscale.at[k], lsgot.at[k], ls_send.at[k], ls_recv.at[k], (me_s, i)))
-        lcopies[-2].start()
-        lcopies[-1].start()
+        lcopies[k] = (
+            send(lpart.at[k], lgot.at[k], l_send.at[k], l_recv.at[k], (me_s, i)),
+            send(lscale.at[k], lsgot.at[k], ls_send.at[k], ls_recv.at[k], (me_s, i)),
+        )
+        for c in lcopies[k]:
+            c.start()
 
     def right(k):
         z = peer_z(k + 1)
@@ -277,19 +297,21 @@
         zcopies[-2].start()
         zcopies[-1].start()
 
+    left(nt - 1)
     right(0)
-    left(1)
+    if nt > 2:
+        left(nt - 2)
     for k in range(1, nz):
         right(k)
         along_z(k - 1)
-        if k + 1 < nt:
-            left(k + 1)
-    for k in range(nz + 1, nt):
-        left(k)
+        if k + 2 < nt:
+            left(nt - 2 - k)
+    for k in range(nz + 2, nt):
+        left(nt - k)
     total = dot(mix[me_t], tr[...].reshape(cols, d), NN) * SCALE
     for k in range(1, nt):
-        lcopies[2 * k - 2].wait()
-        lcopies[2 * k - 1].wait()
+        for c in lcopies[k]:
+            c.wait()
         total = total + decode(lgot[k], lsgot[k])
     out_s[...] = total
     xcopies[nz - 1].wait()

time: 118 us -> 117 us (level)
    pallas_call x1, Pallas kernels: 112 us -> 111 us  [per_device(): pl.pallas_call(functools.partial(body, ns, nt), out_shape=(jax.ShapeDtype...]
where the time goes in v3:
time: 117 us; the launch traced here: 116 us
  Pallas kernels  111 us (95%)
  local copies, waits for them, and re-layouts  4.92 us (4%)
    pallas_call x1, Pallas kernels, per_device(): pl.pallas_call(functools.partial(body, ns, nt), out_shape=(jax.ShapeDtype...  111 us
    unnamed x10, local copies, waits for them, and re-layouts  4.92 us

profile of v3, /device:TPU:0, one launch (start us, length us, event | category | flops | bytes accessed | tf_op | source)
XLA Modules:
  0.0 116.1 jit_solution(6835371893828587593)
XLA Ops:
  0.6 0.0 copy-start
  0.6 1.0 copy-done
  1.6 0.0 copy-start.1
  1.6 0.9 copy-done.1
  2.6 0.0 copy-start.2
  2.6 0.7 copy-done.2
  3.2 0.0 copy-start.3
  3.2 0.7 copy-done.3
  3.9 110.6 %shard_map.59 = (f32[256,768]{1,0:T(8,128)S(1)}, f32[128,768]{1,0:T(8,128)S(1)}) custom-call(bf16[256,768]{1,0:T(8,128)(2,1)S(1)} %copy-done, bf16[128,768]{1,0:T(8,128)(2,1)S(1)} %copy-done.1, f32[1,1024]{1,0:T(1,128)S(1)} %bitcast.2, f32[1,1024]{1,0:T(1,128)S(1)} %bitcast.3), custom_call_target="tpu_custom_call" | custom-call | tf_op jit(solution)/shard_map/pallas_call | solution.py:350
  114.5 0.9 copy.8
  115.4 0.7 copy.9
Async XLA Ops:
  0.6 1.0 copy-start
  1.6 0.9 copy-start.1
  2.6 0.7 copy-start.2
  3.2 0.7 copy-start.3
